TPU v7x, 32 devices: a whole 2x2x4 slice. The times are simulated.
32 devices in a mesh: groups: 2 (over y), res: 4 (over z), blk: 2 (over x), ch: 2 (over core).
Axes of the slice: x: 2, y: 2, z: 4, core: 2. Of those that a mesh axis runs over, the one named last changes fastest.
Arguments:
- single: bfloat16 [16384, 384], P(('groups', 'res')), parts along dimension 0, may hold values from -6 to 6
- frames: float32 [12, 16384], P(None, ('groups', 'res')), parts along dimension 1
- teacher: float32 [12, 16384], P(None, ('groups', 'res')), parts along dimension 1
- res_mask: int32 [16384], P(('groups', 'res')), parts along dimension 0, may hold values 0 or 1
- chain_ids: int32 [16384], P(('groups', 'res')), parts along dimension 0, may hold values from 0 to 31, never falling along the last dimension, each value on 1 to 512 neighbouring positions
- block_pairs: int32 [16, 12, 2], P('groups'), parts along dimension 0, may hold values from 0 to 63, as said below
- w_left: bfloat16 [384, 128], replicated, may hold values from -0.3125 to 0.3125
- w_right: bfloat16 [384, 128], replicated, may hold values from -0.3125 to 0.3125
- w_value: bfloat16 [384, 128], replicated, may hold values from -0.3125 to 0.3125
- w_pair: bfloat16 [128, 128], P(None, 'ch'), may hold values from -0.5 to 0.5
- pair_bias: float32 [128], P('ch'), may hold values from -3 to 3
- gate_vec: float32 [128], P('ch'), may hold values from -1 to 1
- w_out: bfloat16 [128, 384], replicated, may hold values from -0.5 to 0.5
Outputs:
- updated: bfloat16 [16384, 384], P(('groups', 'res')), parts along dimension 0
- pair_fape: float32 [192], P(('groups', 'res', 'blk')), parts along dimension 0
There are 2 independent parts, one for each index of `groups`. A program takes and returns all parts, laid end to end along the dimension named above; an argument that names none is the same for every part. Nothing has to cross between parts.
Inputs may be any that keep to these rules, and one draw needn't show every extreme that they name: block_pairs[o,p,0] lies in blocks (o // 2) * 16 to (o // 2 + 1) * 16 - 1. Among the 12 pairs of one owner at most 4 have their second block in one run of blocks k * 16 to (k+1) * 16 - 1, and in every draw each owner has exactly 4 in one such run.
All inputs are finite; a program needn't handle non-finite values. No bound on the sum of `res_mask` on one device may be relied on, other than what follows from the above.
Results may differ from a plain program's by a relative error of at most 0.0059.
Values may be sent and summed in bfloat16 or wider, within the bound.
A program may use at most 64 MiB of HBM per device.

v0:
```python
import jax
import jax.numpy as jnp
from jax import lax
from jax.sharding import PartitionSpec as P

BLOCK = 128


def tile_logit(near_left, far_right, w_pair, pair_bias, gate_vec):
    outer_prod = (
        near_left.astype(jnp.float32)[:, :, None] * far_right.astype(jnp.float32).T[None, :, :]
    ).astype(jnp.bfloat16)
    pair_act = jnp.einsum("kc,akb->acb", w_pair, outer_prod, preferred_element_type=jnp.float32)
    pair_act = pair_act + pair_bias[None, :, None]
    return jnp.einsum(
        "c,acb->ab", gate_vec, jnp.maximum(pair_act, 0.0), precision=lax.Precision.HIGHEST
    )


def local_coords(geo_near, geo_far, offset):
    coords = []
    for axis_k in range(3):
        summed = jnp.zeros(
            geo_near.shape[:-2] + (geo_near.shape[-1], geo_far.shape[-1]), jnp.float32
        )
        for axis_m in range(3):
            gap_vec = (
                geo_far[..., offset + 9 + axis_m, None, :]
                - geo_near[..., offset + 9 + axis_m, :, None]
            )
            summed = summed + geo_near[..., offset + 3 * axis_m + axis_k, :, None] * gap_vec
        coords.append(summed)
    return coords


def finish(logit, value_near, value_far, geo_near, geo_far):
    live = geo_near[..., 24, :, None] * geo_far[..., 24, None, :]
    live = live * (geo_near[..., 25, :, None] != geo_far[..., 25, None, :]).astype(jnp.float32)
    weight = jax.nn.sigmoid(logit) * live
    weight_low = weight.astype(jnp.bfloat16)
    scale = BLOCK ** (-0.5)
    to_second = jnp.einsum(
        "pab,pac->pbc", weight_low, value_near, preferred_element_type=jnp.float32
    )
    to_second = (to_second * scale).astype(jnp.bfloat16)
    to_first = jnp.einsum("pab,pbc->pac", weight_low, value_far, preferred_element_type=jnp.float32)
    to_first = (to_first * scale).astype(jnp.bfloat16)
    pred_coords = local_coords(geo_near, geo_far, 0)
    true_coords = local_coords(geo_near, geo_far, 12)
    dist_sq = jnp.zeros_like(weight)
    for axis_k in range(3):
        dist_sq = dist_sq + (pred_coords[axis_k] - true_coords[axis_k]) ** 2
    clipped = jnp.minimum(jnp.sqrt(dist_sq + 0.0001), 10.0)
    fape_value = jnp.sum(weight * clipped, axis=(1, 2)) / (BLOCK * BLOCK)
    return (fape_value, to_first, to_second)


def shards(
    single,
    frames,
    teacher,
    res_mask,
    chain_ids,
    block_pairs,
    w_left,
    w_right,
    w_value,
    w_pair,
    pair_bias,
    gate_vec,
    w_out,
):
    res_count = lax.axis_size("res")
    blk_count = lax.axis_size("blk")
    res_rank = lax.axis_index("res")
    blk_rank = lax.axis_index("blk")
    row_count = single.shape[0]
    feat_width = single.shape[1]
    blocks_here = row_count // BLOCK
    pair_dev = block_pairs.shape[1]
    capacity = 1 + (pair_dev + res_count - 2) // res_count
    msg_width = w_value.shape[1]
    owner_table = block_pairs.reshape(res_count, blk_count, pair_dev, 2)
    column_pairs = lax.dynamic_index_in_dim(owner_table, blk_rank, 1, keepdims=False)
    own_pairs = lax.dynamic_index_in_dim(column_pairs, res_rank, 0, keepdims=False)
    wanted_ids = column_pairs[:, :, 1]
    hit_flags = (wanted_ids // blocks_here == res_rank).astype(jnp.int32)
    hit_rank = jnp.cumsum(hit_flags, axis=1) - 1
    slot_ids = jnp.arange(capacity, dtype=jnp.int32)
    picked = hit_flags[:, None, :] * (hit_rank[:, None, :] == slot_ids[None, :, None]).astype(
        jnp.int32
    )
    send_local = jnp.sum(
        picked * (wanted_ids - res_rank * blocks_here)[:, None, :], axis=2
    ).reshape(-1)
    send_valid = jnp.sum(picked, axis=2).reshape(-1)
    geometry = jnp.concatenate(
        [
            frames,
            teacher,
            res_mask[None, :].astype(jnp.float32),
            chain_ids[None, :].astype(jnp.float32),
        ],
        axis=0,
    )
    geo_blocks = geometry.reshape(26, blocks_here, BLOCK).transpose(1, 0, 2)
    geo_send = jnp.take(geo_blocks, send_local, axis=0).reshape(res_count, capacity, 26, BLOCK)
    first_local = own_pairs[:, 0] - res_rank * blocks_here
    source_shard = own_pairs[:, 1] // blocks_here
    pair_index = jnp.arange(pair_dev, dtype=jnp.int32)
    earlier = (source_shard[None, :] == source_shard[:, None]) & (
        pair_index[None, :] < pair_index[:, None]
    )
    recv_slot = source_shard * capacity + jnp.sum(earlier.astype(jnp.int32), axis=1)
    single_blocks = single.reshape(blocks_here, BLOCK, feat_width)
    row_send = jnp.take(single_blocks, send_local, axis=0).reshape(
        res_count, capacity, BLOCK, feat_width
    )
    row_recv = lax.all_to_all(row_send, "res", split_axis=0, concat_axis=0, tiled=True)
    far_rows = jnp.take(row_recv.reshape(-1, BLOCK, feat_width), recv_slot, axis=0)
    near_rows = jnp.take(single_blocks, first_local, axis=0)
    left_feats = jnp.einsum(
        "pad,dc->pac", near_rows, w_left, preferred_element_type=jnp.float32
    ).astype(jnp.bfloat16)
    value_near = jnp.einsum(
        "pad,dc->pac", near_rows, w_value, preferred_element_type=jnp.float32
    ).astype(jnp.bfloat16)
    right_feats = jnp.einsum(
        "pad,dc->pac", far_rows, w_right, preferred_element_type=jnp.float32
    ).astype(jnp.bfloat16)
    value_far = jnp.einsum(
        "pad,dc->pac", far_rows, w_value, preferred_element_type=jnp.float32
    ).astype(jnp.bfloat16)
    geo_recv = lax.all_to_all(
        geo_send.astype(jnp.bfloat16), "res", split_axis=0, concat_axis=0, tiled=True
    ).astype(geo_send.dtype)
    far_geo = jnp.take(geo_recv.reshape(-1, 26, BLOCK), recv_slot, axis=0)
    near_geo = jnp.take(geo_blocks, first_local, axis=0)

    def tile_step(state_in, tile_inputs):
        return (state_in, tile_logit(tile_inputs[0], tile_inputs[1], w_pair, pair_bias, gate_vec))

    state_out, partial_logits = lax.scan(
        tile_step, jnp.zeros((), jnp.float32), (left_feats, right_feats)
    )
    logits = lax.psum(partial_logits, "ch")
    pair_fape, to_first, to_second = finish(logits, value_near, value_far, near_geo, far_geo)
    back_hot = (
        recv_slot[:, None] == jnp.arange(res_count * capacity, dtype=jnp.int32)[None, :]
    ).astype(jnp.bfloat16)
    back_buffer = jnp.einsum(
        "ps,pbc->sbc", back_hot, to_second, preferred_element_type=jnp.float32
    ).astype(jnp.bfloat16)
    back_buffer = back_buffer.reshape(res_count, capacity, BLOCK, msg_width)
    returned = lax.all_to_all(back_buffer, "res", split_axis=0, concat_axis=0, tiled=True)
    block_index = jnp.arange(blocks_here, dtype=jnp.int32)
    send_hot = ((send_local[:, None] == block_index[None, :]) & (send_valid[:, None] > 0)).astype(
        jnp.bfloat16
    )
    delta_rows = jnp.einsum(
        "sl,sbc->lbc",
        send_hot,
        returned.reshape(-1, BLOCK, msg_width),
        preferred_element_type=jnp.float32,
    )
    near_hot = (first_local[:, None] == block_index[None, :]).astype(jnp.bfloat16)
    delta_rows = delta_rows + jnp.einsum(
        "pl,pac->lac", near_hot, to_first, preferred_element_type=jnp.float32
    )
    delta_rows = delta_rows.reshape(row_count, msg_width)
    summed_rows = lax.psum(delta_rows, "blk")
    updated = (
        single.astype(jnp.float32)
        + jnp.dot(summed_rows.astype(jnp.bfloat16), w_out, preferred_element_type=jnp.float32)
    ).astype(jnp.bfloat16)
    return (updated, pair_fape)


def solution(mesh):
    placed = (
        P(("groups", "res"), None),
        P(None, ("groups", "res")),
        P(None, ("groups", "res")),
        P(("groups", "res")),
        P(("groups", "res")),
        P("groups", None, None),
        P(),
        P(),
        P(),
        P(None, "ch"),
        P("ch"),
        P("ch"),
        P(),
    )
    return jax.shard_map(
        shards,
        mesh=mesh,
        in_specs=placed,
        out_specs=(P(("groups", "res"), None), P(("groups", "res", "blk"))),
        check_vma=False,
    )
```

profile of v0, /device:TPU:0, one launch (start us, length us, event | category | flops | bytes accessed | tf_op | source)
XLA Modules:
  0.0 224.0 jit_solution(8328334812829523707)
XLA Ops:
  7.2 0.7 constant_dynamic-slice_fusion.1
  8.1 0.7 select_reduce_fusion
  8.9 2.3 %gather_fusion = bf16[16,128,384]{2,1,0:T(8,128)(2,1)S(1)} fusion(bf16[16,128,384]{2,1,0:T(8,128)(2,1)} %bitcast.219, s32[1024]{0:T(1024)S(1)} %pad_clamp_fusion.1), kind=kCustom, calls=%fused_computation.4 | custom fusion | bytes 3145792 | tf_op jit(solution)/shard_map/jit(_take)/gather | solution.py:116
  11.3 1.4 broadcast_select_fusion
  12.7 6.4 %all-to-all-start = ((bf16[4,4,128,384]{3,2,1,0:T(8,128)(2,1)}), bf16[4,4,128,384]{3,2,1,0:T(8,128)(2,1)S(1)}, u32[]{:S(2)}, u32[]{:S(2)}) async-start(bf16[4,4,128,384]{3,2,1,0:T(8,128)(2,1)} %broadcast_select_fusion), calls=%async_computation | async-start | bytes 3145728 | tf_op jit(solution)/shard_map/all_to_all | solution.py:119
  19.1 0.7 dynamic-slice_bitcast_fusion
  20.5 1.8 gather_fusion.2
  22.6 1.2 gather_fusion.1
  23.8 1.2 gather_fusion.4
  25.8 1.0 broadcast_select_fusion.10
  28.1 1.7 fusion.42
  29.8 2.6 %convolution_convert_fusion.4 = bf16[12,128,128]{2,1,0:T(8,128)(2,1)} fusion(bf16[12,128,384]{2,1,0:T(8,128)(2,1)} %gather_fusion.2, pred[12]{0:T(512)(128)(4,1)} %copy-done.26, bf16[384,128]{1,0:T(8,128)(2,1)} %param.25), kind=kOutput, calls=%fused_computation.52 | convolution fusion | flops 151781376 | bytes 1671180 | tf_op jit(solution)/shard_map/pad,dc->pac/dot_general | solution.py:122
  32.3 23.7 %all-to-all-done = bf16[4,4,128,384]{3,2,1,0:T(8,128)(2,1)S(1)} async-done(((bf16[4,4,128,384]{3,2,1,0:T(8,128)(2,1)}), bf16[4,4,128,384]{3,2,1,0:T(8,128)(2,1)S(1)}, u32[]{:S(2)}, u32[]{:S(2)}) %all-to-all-start) | async-done | bytes 1572896 | tf_op jit(solution)/shard_map/all_to_all | solution.py:119
  56.1 3.3 %all-to-all-start.1 = ((bf16[4,4,26,128]{3,1,2,0:T(4,128)(2,1)}), bf16[4,4,26,128]{3,1,2,0:T(4,128)(2,1)S(1)}, u32[]{:S(2)}, u32[]{:S(2)}) async-start(bf16[4,4,26,128]{3,1,2,0:T(4,128)(2,1)} %fusion.42), calls=%async_computation.1 | async-start | bytes 212992 | tf_op jit(solution)/shard_map/all_to_all | solution.py:134
  59.4 1.8 gather_fusion.3
  61.2 1.8 convolution_convert_fusion.3
  63.1 79.4 %while.11 = (s32[]{:T(128)}, f32[12,128,128]{2,1,0:T(8,128)}, bf16[12,128,128]{2,1,0:T(8,128)(2,1)}, bf16[12,128,128]{2,1,0:T(8,128)(2,1)S(1)}, bf16[128,64]{0,1...) while((s32[]{:T(128)}, f32[12,128,128]{2,1,0:T(8,128)}, bf16[12,128,128]{2,1,0:T(8,128)(2,1)}, ...), condition=%wide.region_5.7_spmd.clone, body=%wide.region_4.6_spmd.sunk.clone | while | flops 287342592 | bytes 9061461 | solution.py:143
  63.3 0.8 bitcast_convert_fusion.3
  64.1 2.5 %fusion.98 = f32[128,128,64]{1,2,0:T(8,128)S(1)} fusion(f32[128,128]{1,0:T(8,128)S(1)} %convert_bitcast_fusion.3, f32[128,128]{1,0:T(8,128)S(1)} %bitcast_convert_fusion.3, bf16[128,64]{0,1:T(8,128)(2,1)S(1)} %get-tuple-element.198), kind=kOutput, calls=%fused_computation.7.clone.1.clone | convolution fusion | flops 272629760 | bytes 4341760 | tf_op jit(solution)/shard_map/while/body/eval_jaxpr/kc,akb->acb/dot_general | solution.py:13
  66.6 2.5 %fusion.99 = f32[1,128,128]{2,0,1:T(1,128)S(1)} fusion(f32[128,128,64]{1,2,0:T(8,128)S(1)} %fusion.98, f32[64]{0:T(128)S(1)} %get-tuple-element.199, f32[64]{0:T(128)S(1)} %get-tuple-element.200), kind=kOutput, calls=%fused_computation.8.clone.1.clone | convolution fusion | flops 14680064 | bytes 4260352 | tf_op jit(solution)/shard_map/while/body/eval_jaxpr/c,acb->ab/dot_general | solution.py:15
  69.9 0.8 bitcast_convert_fusion.3
  70.7 2.5 %fusion.98 = f32[128,128,64]{1,2,0:T(8,128)S(1)} fusion(f32[128,128]{1,0:T(8,128)S(1)} %convert_bitcast_fusion.3, f32[128,128]{1,0:T(8,128)S(1)} %bitcast_convert_fusion.3, bf16[128,64]{0,1:T(8,128)(2,1)S(1)} %get-tuple-element.198), kind=kOutput, calls=%fused_computation.7.clone.1.clone | convolution fusion | flops 272629760 | bytes 4341760 | tf_op jit(solution)/shard_map/while/body/eval_jaxpr/kc,akb->acb/dot_general | solution.py:13
  73.2 2.5 %fusion.99 = f32[1,128,128]{2,0,1:T(1,128)S(1)} fusion(f32[128,128,64]{1,2,0:T(8,128)S(1)} %fusion.98, f32[64]{0:T(128)S(1)} %get-tuple-element.199, f32[64]{0:T(128)S(1)} %get-tuple-element.200), kind=kOutput, calls=%fused_computation.8.clone.1.clone | convolution fusion | flops 14680064 | bytes 4260352 | tf_op jit(solution)/shard_map/while/body/eval_jaxpr/c,acb->ab/dot_general | solution.py:15
  76.5 0.8 bitcast_convert_fusion.3
  77.3 2.5 %fusion.98 = f32[128,128,64]{1,2,0:T(8,128)S(1)} fusion(f32[128,128]{1,0:T(8,128)S(1)} %convert_bitcast_fusion.3, f32[128,128]{1,0:T(8,128)S(1)} %bitcast_convert_fusion.3, bf16[128,64]{0,1:T(8,128)(2,1)S(1)} %get-tuple-element.198), kind=kOutput, calls=%fused_computation.7.clone.1.clone | convolution fusion | flops 272629760 | bytes 4341760 | tf_op jit(solution)/shard_map/while/body/eval_jaxpr/kc,akb->acb/dot_general | solution.py:13
  79.8 2.5 %fusion.99 = f32[1,128,128]{2,0,1:T(1,128)S(1)} fusion(f32[128,128,64]{1,2,0:T(8,128)S(1)} %fusion.98, f32[64]{0:T(128)S(1)} %get-tuple-element.199, f32[64]{0:T(128)S(1)} %get-tuple-element.200), kind=kOutput, calls=%fused_computation.8.clone.1.clone | convolution fusion | flops 14680064 | bytes 4260352 | tf_op jit(solution)/shard_map/while/body/eval_jaxpr/c,acb->ab/dot_general | solution.py:15
  83.2 0.8 bitcast_convert_fusion.3
  83.9 2.5 %fusion.98 = f32[128,128,64]{1,2,0:T(8,128)S(1)} fusion(f32[128,128]{1,0:T(8,128)S(1)} %convert_bitcast_fusion.3, f32[128,128]{1,0:T(8,128)S(1)} %bitcast_convert_fusion.3, bf16[128,64]{0,1:T(8,128)(2,1)S(1)} %get-tuple-element.198), kind=kOutput, calls=%fused_computation.7.clone.1.clone | convolution fusion | flops 272629760 | bytes 4341760 | tf_op jit(solution)/shard_map/while/body/eval_jaxpr/kc,akb->acb/dot_general | solution.py:13
  86.5 2.5 %fusion.99 = f32[1,128,128]{2,0,1:T(1,128)S(1)} fusion(f32[128,128,64]{1,2,0:T(8,128)S(1)} %fusion.98, f32[64]{0:T(128)S(1)} %get-tuple-element.199, f32[64]{0:T(128)S(1)} %get-tuple-element.200), kind=kOutput, calls=%fused_computation.8.clone.1.clone | convolution fusion | flops 14680064 | bytes 4260352 | tf_op jit(solution)/shard_map/while/body/eval_jaxpr/c,acb->ab/dot_general | solution.py:15
  89.8 0.8 bitcast_convert_fusion.3
  90.5 2.5 %fusion.98 = f32[128,128,64]{1,2,0:T(8,128)S(1)} fusion(f32[128,128]{1,0:T(8,128)S(1)} %convert_bitcast_fusion.3, f32[128,128]{1,0:T(8,128)S(1)} %bitcast_convert_fusion.3, bf16[128,64]{0,1:T(8,128)(2,1)S(1)} %get-tuple-element.198), kind=kOutput, calls=%fused_computation.7.clone.1.clone | convolution fusion | flops 272629760 | bytes 4341760 | tf_op jit(solution)/shard_map/while/body/eval_jaxpr/kc,akb->acb/dot_general | solution.py:13
  93.1 2.5 %fusion.99 = f32[1,128,128]{2,0,1:T(1,128)S(1)} fusion(f32[128,128,64]{1,2,0:T(8,128)S(1)} %fusion.98, f32[64]{0:T(128)S(1)} %get-tuple-element.199, f32[64]{0:T(128)S(1)} %get-tuple-element.200), kind=kOutput, calls=%fused_computation.8.clone.1.clone | convolution fusion | flops 14680064 | bytes 4260352 | tf_op jit(solution)/shard_map/while/body/eval_jaxpr/c,acb->ab/dot_general | solution.py:15
  96.4 0.8 bitcast_convert_fusion.3
  97.2 2.5 %fusion.98 = f32[128,128,64]{1,2,0:T(8,128)S(1)} fusion(f32[128,128]{1,0:T(8,128)S(1)} %convert_bitcast_fusion.3, f32[128,128]{1,0:T(8,128)S(1)} %bitcast_convert_fusion.3, bf16[128,64]{0,1:T(8,128)(2,1)S(1)} %get-tuple-element.198), kind=kOutput, calls=%fused_computation.7.clone.1.clone | convolution fusion | flops 272629760 | bytes 4341760 | tf_op jit(solution)/shard_map/while/body/eval_jaxpr/kc,akb->acb/dot_general | solution.py:13
  99.7 2.5 %fusion.99 = f32[1,128,128]{2,0,1:T(1,128)S(1)} fusion(f32[128,128,64]{1,2,0:T(8,128)S(1)} %fusion.98, f32[64]{0:T(128)S(1)} %get-tuple-element.199, f32[64]{0:T(128)S(1)} %get-tuple-element.200), kind=kOutput, calls=%fused_computation.8.clone.1.clone | convolution fusion | flops 14680064 | bytes 4260352 | tf_op jit(solution)/shard_map/while/body/eval_jaxpr/c,acb->ab/dot_general | solution.py:15
  103.0 0.8 bitcast_convert_fusion.3
  103.8 2.5 %fusion.98 = f32[128,128,64]{1,2,0:T(8,128)S(1)} fusion(f32[128,128]{1,0:T(8,128)S(1)} %convert_bitcast_fusion.3, f32[128,128]{1,0:T(8,128)S(1)} %bitcast_convert_fusion.3, bf16[128,64]{0,1:T(8,128)(2,1)S(1)} %get-tuple-element.198), kind=kOutput, calls=%fused_computation.7.clone.1.clone | convolution fusion | flops 272629760 | bytes 4341760 | tf_op jit(solution)/shard_map/while/body/eval_jaxpr/kc,akb->acb/dot_general | solution.py:13
  106.3 2.5 %fusion.99 = f32[1,128,128]{2,0,1:T(1,128)S(1)} fusion(f32[128,128,64]{1,2,0:T(8,128)S(1)} %fusion.98, f32[64]{0:T(128)S(1)} %get-tuple-element.199, f32[64]{0:T(128)S(1)} %get-tuple-element.200), kind=kOutput, calls=%fused_computation.8.clone.1.clone | convolution fusion | flops 14680064 | bytes 4260352 | tf_op jit(solution)/shard_map/while/body/eval_jaxpr/c,acb->ab/dot_general | solution.py:15
  109.6 0.8 bitcast_convert_fusion.3
  110.4 2.5 %fusion.98 = f32[128,128,64]{1,2,0:T(8,128)S(1)} fusion(f32[128,128]{1,0:T(8,128)S(1)} %convert_bitcast_fusion.3, f32[128,128]{1,0:T(8,128)S(1)} %bitcast_convert_fusion.3, bf16[128,64]{0,1:T(8,128)(2,1)S(1)} %get-tuple-element.198), kind=kOutput, calls=%fused_computation.7.clone.1.clone | convolution fusion | flops 272629760 | bytes 4341760 | tf_op jit(solution)/shard_map/while/body/eval_jaxpr/kc,akb->acb/dot_general | solution.py:13
  112.9 2.5 %fusion.99 = f32[1,128,128]{2,0,1:T(1,128)S(1)} fusion(f32[128,128,64]{1,2,0:T(8,128)S(1)} %fusion.98, f32[64]{0:T(128)S(1)} %get-tuple-element.199, f32[64]{0:T(128)S(1)} %get-tuple-element.200), kind=kOutput, calls=%fused_computation.8.clone.1.clone | convolution fusion | flops 14680064 | bytes 4260352 | tf_op jit(solution)/shard_map/while/body/eval_jaxpr/c,acb->ab/dot_general | solution.py:15
  116.2 0.8 bitcast_convert_fusion.3
  117.0 2.5 %fusion.98 = f32[128,128,64]{1,2,0:T(8,128)S(1)} fusion(f32[128,128]{1,0:T(8,128)S(1)} %convert_bitcast_fusion.3, f32[128,128]{1,0:T(8,128)S(1)} %bitcast_convert_fusion.3, bf16[128,64]{0,1:T(8,128)(2,1)S(1)} %get-tuple-element.198), kind=kOutput, calls=%fused_computation.7.clone.1.clone | convolution fusion | flops 272629760 | bytes 4341760 | tf_op jit(solution)/shard_map/while/body/eval_jaxpr/kc,akb->acb/dot_general | solution.py:13
  119.5 2.5 %fusion.99 = f32[1,128,128]{2,0,1:T(1,128)S(1)} fusion(f32[128,128,64]{1,2,0:T(8,128)S(1)} %fusion.98, f32[64]{0:T(128)S(1)} %get-tuple-element.199, f32[64]{0:T(128)S(1)} %get-tuple-element.200), kind=kOutput, calls=%fused_computation.8.clone.1.clone | convolution fusion | flops 14680064 | bytes 4260352 | tf_op jit(solution)/shard_map/while/body/eval_jaxpr/c,acb->ab/dot_general | solution.py:15
  122.9 0.8 bitcast_convert_fusion.3
  123.6 2.5 %fusion.98 = f32[128,128,64]{1,2,0:T(8,128)S(1)} fusion(f32[128,128]{1,0:T(8,128)S(1)} %convert_bitcast_fusion.3, f32[128,128]{1,0:T(8,128)S(1)} %bitcast_convert_fusion.3, bf16[128,64]{0,1:T(8,128)(2,1)S(1)} %get-tuple-element.198), kind=kOutput, calls=%fused_computation.7.clone.1.clone | convolution fusion | flops 272629760 | bytes 4341760 | tf_op jit(solution)/shard_map/while/body/eval_jaxpr/kc,akb->acb/dot_general | solution.py:13
  126.2 2.5 %fusion.99 = f32[1,128,128]{2,0,1:T(1,128)S(1)} fusion(f32[128,128,64]{1,2,0:T(8,128)S(1)} %fusion.98, f32[64]{0:T(128)S(1)} %get-tuple-element.199, f32[64]{0:T(128)S(1)} %get-tuple-element.200), kind=kOutput, calls=%fused_computation.8.clone.1.clone | convolution fusion | flops 14680064 | bytes 4260352 | tf_op jit(solution)/shard_map/while/body/eval_jaxpr/c,acb->ab/dot_general | solution.py:15
  129.5 0.8 bitcast_convert_fusion.3
  130.3 2.5 %fusion.98 = f32[128,128,64]{1,2,0:T(8,128)S(1)} fusion(f32[128,128]{1,0:T(8,128)S(1)} %convert_bitcast_fusion.3, f32[128,128]{1,0:T(8,128)S(1)} %bitcast_convert_fusion.3, bf16[128,64]{0,1:T(8,128)(2,1)S(1)} %get-tuple-element.198), kind=kOutput, calls=%fused_computation.7.clone.1.clone | convolution fusion | flops 272629760 | bytes 4341760 | tf_op jit(solution)/shard_map/while/body/eval_jaxpr/kc,akb->acb/dot_general | solution.py:13
  132.8 2.5 %fusion.99 = f32[1,128,128]{2,0,1:T(1,128)S(1)} fusion(f32[128,128,64]{1,2,0:T(8,128)S(1)} %fusion.98, f32[64]{0:T(128)S(1)} %get-tuple-element.199, f32[64]{0:T(128)S(1)} %get-tuple-element.200), kind=kOutput, calls=%fused_computation.8.clone.1.clone | convolution fusion | flops 14680064 | bytes 4260352 | tf_op jit(solution)/shard_map/while/body/eval_jaxpr/c,acb->ab/dot_general | solution.py:15
  136.1 0.8 bitcast_convert_fusion.3
  136.9 2.5 %fusion.98 = f32[128,128,64]{1,2,0:T(8,128)S(1)} fusion(f32[128,128]{1,0:T(8,128)S(1)} %convert_bitcast_fusion.3, f32[128,128]{1,0:T(8,128)S(1)} %bitcast_convert_fusion.3, bf16[128,64]{0,1:T(8,128)(2,1)S(1)} %get-tuple-element.198), kind=kOutput, calls=%fused_computation.7.clone.1.clone | convolution fusion | flops 272629760 | bytes 4341760 | tf_op jit(solution)/shard_map/while/body/eval_jaxpr/kc,akb->acb/dot_general | solution.py:13
  139.4 2.5 %fusion.99 = f32[1,128,128]{2,0,1:T(1,128)S(1)} fusion(f32[128,128,64]{1,2,0:T(8,128)S(1)} %fusion.98, f32[64]{0:T(128)S(1)} %get-tuple-element.199, f32[64]{0:T(128)S(1)} %get-tuple-element.200), kind=kOutput, calls=%fused_computation.8.clone.1.clone | convolution fusion | flops 14680064 | bytes 4260352 | tf_op jit(solution)/shard_map/while/body/eval_jaxpr/c,acb->ab/dot_general | solution.py:15
  146.6 0.7 gather_fusion.5
  147.3 0.8 broadcast_select_fusion.9
  151.7 11.7 %all-reduce.3.cloned.1.call-done = f32[12,128,128]{2,1,0:T(8,128)} async-done(((f32[12,128,128]{2,1,0:T(8,128)}), f32[12,128,128]{2,1,0:T(8,128)}) %all-reduce.3.cloned.1.call-update) | async-done | bytes 786448 | tf_op jit(solution)/shard_map/psum | solution.py:146
  163.4 2.0 fusion.12
  165.8 1.0 copy.48
  166.8 4.9 %all-to-all-start.2 = ((bf16[4,4,128,128]{3,1,2,0:T(4,128)(2,1)}), bf16[4,4,128,128]{3,1,2,0:T(4,128)(2,1)S(1)}, u32[]{:S(2)}, u32[]{:S(2)}) async-start(bf16[4,4,128,128]{3,1,2,0:T(4,128)(2,1)} %copy.48), calls=%async_computation.2 | async-start | bytes 1048576 | tf_op jit(solution)/shard_map/all_to_all | solution.py:155
  171.7 7.5 %fusion.38 = f32[12]{0:T(128)S(1)} fusion(f32[12,128]{1,0:T(8,128)S(1)} %bitcast.233, f32[12,128]{1,0:T(8,128)S(1)} %bitcast.234, f32[12,128]{1,0:T(8,128)S(1)} %bitcast.235, f32[12,128]{1,0:T(8,128)S(1)} %bitcast.236, f32[12,128]{1,0:T(8,128)S(1)} %bitcast.240, f32[12,128]{1,0:T(8,128)S(1)} %bitcast.244, f32[12,128]{1,0:T(8,128)S(1)} %bitcast.245, ...), kind=kLoop, calls=%fused_computation.80 | loop fusion | flops 10813428 | bytes 995376 | tf_op jit(solution)/shard_map/reduce_sum | solution.py:54
  179.7 2.7 %fusion.13 = bf16[12,128,128]{2,1,0:T(8,128)(2,1)} fusion(bf16[12,128,384]{2,1,0:T(8,128)(2,1)S(1)} %copy-done.3, pred[12]{0:T(512)(128)(4,1)} %copy-done.25, bf16[384,128]{1,0:T(8,128)(2,1)} %param.27, f32[12,128,128]{2,1,0:T(8,128)} %all-reduce.3.cloned.1.call-done, f32[12,128]{1,0:T(8,128)} %bitcast.265, f32[12,128]{1,0:T(8,128)S(1)} %bitcast.239, ...), kind=kOutput, calls=%fused_computation.48 | convolution fusion | flops 204079104 | bytes 2482188 | tf_op jit(solution)/shard_map/pab,pbc->pac/dot_general | solution.py:46
  182.4 4.2 %all-to-all-done.2 = bf16[4,4,128,128]{3,1,2,0:T(4,128)(2,1)S(1)} async-done(((bf16[4,4,128,128]{3,1,2,0:T(4,128)(2,1)}), bf16[4,4,128,128]{3,1,2,0:T(4,128)(2,1)S(1)}, u32[]{:S(2)}, u32[]{:S(2)}) %all-to-all-start.2) | async-done | bytes 524320 | tf_op jit(solution)/shard_map/all_to_all | solution.py:155
  187.8 27.6 %all-reduce.4 = bf16[2048,128]{1,0:T(8,128)(2,1)S(1)} all-reduce(f32[2048,128]{1,0:T(8,128)S(1)} %bitcast.224), channel_id=1, replica_groups=mesh['groups'=2,'res'=4,'blk'=2,'ch'=2] {'blk'}, use_global_device_ids=true, to_apply=%region_7.10 | all-reduce | flops 262144 | bytes 1572864 | tf_op jit(solution)/shard_map/psum | solution.py:171
  215.5 1.7 add_convert_fusion
  (184 shorter events, 21.7 us)
Async XLA Ops:
  7.2 208.3 %copy-start = (bf16[128,384]{1,0:T(8,128)(2,1)S(1)}, bf16[128,384]{1,0:T(8,128)(2,1)}, u32[]{:S(2)}) copy-start(bf16[128,384]{1,0:T(8,128)(2,1)} %param.31) | copy-start | bytes 294916
  8.9 2.3 %copy-start.19 = (pred[4,4]{1,0:T(4,128)(4,1)}, pred[4,4]{1,0:T(4,128)(4,1)S(1)}, u32[]{:S(2)}) copy-start(pred[4,4]{1,0:T(4,128)(4,1)S(1)} %compare_and_fusion.2) | copy-start | bytes 52
  12.7 7.8 %copy-start.1 = (bf16[2048,384]{1,0:T(8,128)(2,1)S(1)}, bf16[2048,384]{1,0:T(8,128)(2,1)}, u32[]{:S(2)}) copy-start(bf16[2048,384]{1,0:T(8,128)(2,1)} %param.19) | copy-start | bytes 4718596
  12.7 43.4 %all-to-all-start = ((bf16[4,4,128,384]{3,2,1,0:T(8,128)(2,1)}), bf16[4,4,128,384]{3,2,1,0:T(8,128)(2,1)S(1)}, u32[]{:S(2)}, u32[]{:S(2)}) async-start(bf16[4,4,128,384]{3,2,1,0:T(8,128)(2,1)} %broadcast_select_fusion), calls=%async_computation | async-start | bytes 3145728 | tf_op jit(solution)/shard_map/all_to_all | solution.py:119
  19.1 3.2 %copy-start.6 = (f32[12,2048]{1,0:T(8,128)S(1)}, f32[12,2048]{1,0:T(8,128)}, u32[]{:S(2)}) copy-start(f32[12,2048]{1,0:T(8,128)} %param.20) | copy-start | bytes 294916
  19.1 3.3 %copy-start.7 = (f32[12,2048]{1,0:T(8,128)S(1)}, f32[12,2048]{1,0:T(8,128)}, u32[]{:S(2)}) copy-start(f32[12,2048]{1,0:T(8,128)} %param.21) | copy-start | bytes 294916
  19.8 5.2 %copy-start.22 = (s32[12,2]{0,1:T(2,128)}, s32[12,2]{0,1:T(2,128)S(1)}, u32[]{:S(2)}) copy-start(s32[12,2]{0,1:T(2,128)S(1)} %dynamic-slice_bitcast_fusion) | copy-start | bytes 292
  19.8 0.6 copy-start.20
  19.9 5.9 %copy-start.26 = (pred[12]{0:T(512)(128)(4,1)}, pred[12]{0:T(512)(128)(4,1)S(1)}, u32[]{:S(2)}) copy-start(pred[12]{0:T(512)(128)(4,1)S(1)} %get-tuple-element.81) | copy-start | bytes 40
  20.4 2.0 copy-start.16
  20.5 2.0 copy-start.17
  25.2 0.6 copy-start.28
  25.8 35.4 %copy-start.25 = (pred[12]{0:T(512)(128)(4,1)}, pred[12]{0:T(512)(128)(4,1)S(1)}, u32[]{:S(2)}) copy-start(pred[12]{0:T(512)(128)(4,1)S(1)} %get-tuple-element.79) | copy-start | bytes 40
  25.8 33.6 %copy-start.18 = (s32[1024]{0:T(1024)}, s32[1024]{0:T(1024)S(1)}, u32[]{:S(2)}) copy-start(s32[1024]{0:T(1024)S(1)} %pad_clamp_fusion) | copy-start | bytes 12292
  56.1 90.5 %all-to-all-start.1 = ((bf16[4,4,26,128]{3,1,2,0:T(4,128)(2,1)}), bf16[4,4,26,128]{3,1,2,0:T(4,128)(2,1)S(1)}, u32[]{:S(2)}, u32[]{:S(2)}) async-start(bf16[4,4,26,128]{3,1,2,0:T(4,128)(2,1)} %fusion.42), calls=%async_computation.1 | async-start | bytes 212992 | tf_op jit(solution)/shard_map/all_to_all | solution.py:134
  59.4 104.0 %all-reduce.3.cloned.1.call-start = ((), (), s32[]{:S(2)}) async-start(), calls=%async_computation.3 | async-start | bytes 1572864 | tf_op jit(solution)/shard_map/psum | solution.py:146
  61.2 1.9 copy-start.5
  61.2 1.9 copy-start.13
  61.2 1.9 copy-start.14
  63.1 79.5 %copy-start.15 = (s32[4,4]{1,0:T(4,128)S(1)}, s32[4,4]{1,0:T(4,128)}, u32[]{:S(2)}) copy-start(s32[4,4]{1,0:T(4,128)} %get-tuple-element.63) | copy-start | bytes 196
  63.1 80.2 %copy-start.12 = (f32[12,1,128]{2,1,0:T(1,128)S(1)}, f32[12,1,128]{2,1,0:T(1,128)}, u32[]{:S(2)}) copy-start(f32[12,1,128]{2,1,0:T(1,128)} %get-tuple-element.97) | copy-start | bytes 18436
  63.1 80.3 %copy-start.11 = (f32[12,1,128]{2,1,0:T(1,128)S(1)}, f32[12,1,128]{2,1,0:T(1,128)}, u32[]{:S(2)}) copy-start(f32[12,1,128]{2,1,0:T(1,128)} %get-tuple-element.111) | copy-start | bytes 18436
  63.1 80.3 %copy-start.10 = (f32[12,1,128]{2,1,0:T(1,128)S(1)}, f32[12,1,128]{2,1,0:T(1,128)}, u32[]{:S(2)}) copy-start(f32[12,1,128]{2,1,0:T(1,128)} %get-tuple-element.112) | copy-start | bytes 18436
  63.1 83.4 %copy-start.23 = (s32[12,2]{0,1:T(2,128)S(1)}, s32[12,2]{0,1:T(2,128)}, u32[]{:S(2)}) copy-start(s32[12,2]{0,1:T(2,128)} %copy-done.22) | copy-start | bytes 292
  63.1 83.4 %copy-start.29 = (s32[12]{0:T(128)S(1)}, s32[12]{0:T(128)}, u32[]{:S(2)}) copy-start(s32[12]{0:T(128)} %copy-done.28) | copy-start | bytes 148
  142.6 20.8 %copy-start.2 = (bf16[12,128,384]{2,1,0:T(8,128)(2,1)S(1)}, bf16[12,128,384]{2,1,0:T(8,128)(2,1)}, u32[]{:S(2)}) copy-start(bf16[12,128,384]{2,1,0:T(8,128)(2,1)} %gather_fusion.2) | copy-start | bytes 3538948
  151.6 13.8 %copy-start.8 = (f32[12,1,128]{2,0,1:T(8,128)}, f32[12,1,128]{2,0,1:T(8,128)S(1)}, u32[]{:S(2)}) copy-start(f32[12,1,128]{2,0,1:T(8,128)S(1)} %copy.163) | copy-start | bytes 18436
  151.7 13.8 %copy-start.9 = (f32[12,1,128]{2,0,1:T(8,128)}, f32[12,1,128]{2,0,1:T(8,128)S(1)}, u32[]{:S(2)}) copy-start(f32[12,1,128]{2,0,1:T(8,128)S(1)} %copy.165) | copy-start | bytes 18436
  165.8 13.9 %copy-start.3 = (bf16[12,128,384]{2,1,0:T(8,128)(2,1)S(1)}, bf16[12,128,384]{2,1,0:T(8,128)(2,1)}, u32[]{:S(2)}) copy-start(bf16[12,128,384]{2,1,0:T(8,128)(2,1)} %gather_fusion.3) | copy-start | bytes 3538948
  166.8 19.8 %all-to-all-start.2 = ((bf16[4,4,128,128]{3,1,2,0:T(4,128)(2,1)}), bf16[4,4,128,128]{3,1,2,0:T(4,128)(2,1)S(1)}, u32[]{:S(2)}, u32[]{:S(2)}) async-start(bf16[4,4,128,128]{3,1,2,0:T(4,128)(2,1)} %copy.48), calls=%async_computation.2 | async-start | bytes 1048576 | tf_op jit(solution)/shard_map/all_to_all | solution.py:155
  179.7 7.1 %copy-start.24 = (s32[16]{0:T(128)S(1)}, s32[16]{0:T(128)}, u32[]{:S(2)}) copy-start(s32[16]{0:T(128)} %eq.90) | copy-start | bytes 196
  179.7 7.1 %copy-start.27 = (pred[16]{0:T(512)(128)(4,1)S(1)}, pred[16]{0:T(512)(128)(4,1)}, u32[]{:S(2)}) copy-start(pred[16]{0:T(512)(128)(4,1)} %gt.12) | copy-start | bytes 52
  182.4 4.7 %copy-start.4 = (bf16[12,128,128]{2,1,0:T(8,128)(2,1)S(1)}, bf16[12,128,128]{2,1,0:T(8,128)(2,1)}, u32[]{:S(2)}) copy-start(bf16[12,128,128]{2,1,0:T(8,128)(2,1)} %fusion.13) | copy-start | bytes 1179652
  182.4 4.7 %copy-start.21 = (s32[12]{0:T(128)S(1)}, s32[12]{0:T(128)}, u32[]{:S(2)}) copy-start(s32[12]{0:T(128)} %copy-done.20) | copy-start | bytes 148
Sparse Core Ops, SparseCore 0:
  142.7 20.5 all-reduce.2
where the time goes:
time: 225 us; the launch traced here: 224 us
  matrix products  72.7 us (32%)
  waiting for transfers between devices  39.6 us (18%)
  local copies, waits for them, and re-layouts  31 us (14%)
  blocking collectives  27.6 us (12%)
  other arithmetic  23.4 us (10%)
  starting transfers between devices  14.7 us (7%)
  between operations  14.7 us (7%)
    dot_general x12, matrix products, tile_logit(): jnp.einsum('c,acb->ab', gate_vec, jnp.maximum(pair_act, 0.0), precision=l...  30.6 us
    dot_general x12, matrix products, tile_logit(): jnp.einsum('kc,akb->acb', w_pair, outer_prod, preferred_element_type=jnp....  30.3 us
    psum x1, blocking collectives, shards(): summed_rows = lax.psum(delta_rows, 'blk')  27.6 us
    all_to_all x1, waiting for transfers between devices, shards(): lax.all_to_all(row_send, 'res', split_axis=0, concat_axis=0, tiled=True)  23.7 us
    psum x1, waiting for transfers between devices, shards(): logits = lax.psum(partial_logits, 'ch')  11.7 us
    convert_element_type x12, other arithmetic, tile_logit(): near_left.astype(jnp.float32)[:, :, None]  9.25 us
    dynamic_update_slice x12, local copies, waits for them, and re-layouts, shards(): lax.scan(tile_step, jnp.zeros((), jnp.float32), (left_feats, right_feats))  7.54 us
    reduce_sum x1, other arithmetic, finish(): fape_value = jnp.sum(weight * clipped, axis=(1, 2)) / (BLOCK * BLOCK)  7.52 us
  transfers between devices with their start and end apart: 4, of which 3 were waited for; matrix products, arithmetic and copies ran while one was open for 51% of the time, Pallas kernels for 0%

commit v1 on v0

--- a/solution.py
+++ b/solution.py
@@ -143,7 +143,7 @@
     state_out, partial_logits = lax.scan(
         tile_step, jnp.zeros((), jnp.float32), (left_feats, right_feats)
     )
-    logits = lax.psum(partial_logits, "ch")
+    logits = jnp.sum(lax.all_gather(partial_logits, "ch"), axis=0)
     pair_fape, to_first, to_second = finish(logits, value_near, value_far, near_geo, far_geo)
     back_hot = (
         recv_slot[:, None] == jnp.arange(res_count * capacity, dtype=jnp.int32)[None, :]

time: 225 us -> 217 us (0.964)
  local copies, waits for them, and re-layouts: 31 us -> 21.4 us
    psum x1 -> x0, waiting for transfers between devices: 11.7 us -> none  [shards(): logits = lax.psum(partial_logits, 'ch')]
    all_gather x0 -> x1, waiting for transfers between devices: none -> 9.9 us  [shards(): logits = jnp.sum(lax.all_gather(partial_logits, 'ch'), axis=0)]
    unnamed x96 -> x60, local copies, waits for them, and re-layouts: 7.31 us -> 0.2 us
  transfers between devices with their start and end apart: 4 -> 4, of which waited for: 3 -> 3; matrix products, arithmetic and copies ran while one was open for 51% -> 48% of each run, Pallas kernels for 0% -> 0%
where the time goes in v1:
time: 217 us; the launch traced here: 216 us
  matrix products  72.2 us (33%)
  waiting for transfers between devices  41.6 us (19%)
  blocking collectives  27.7 us (13%)
  other arithmetic  23.3 us (11%)
  local copies, waits for them, and re-layouts  21.4 us (10%)
  starting transfers between devices  14.7 us (7%)
  between operations  14.7 us (7%)
    dot_general x12, matrix products, tile_logit(): jnp.einsum('c,acb->ab', gate_vec, jnp.maximum(pair_act, 0.0), precision=l...  30.6 us
    dot_general x12, matrix products, tile_logit(): jnp.einsum('kc,akb->acb', w_pair, outer_prod, preferred_element_type=jnp....  30.3 us
    psum x1, blocking collectives, shards(): summed_rows = lax.psum(delta_rows, 'blk')  27.7 us
    all_to_all x1, waiting for transfers between devices, shards(): lax.all_to_all(row_send, 'res', split_axis=0, concat_axis=0, tiled=True)  25.5 us
    all_gather x1, waiting for transfers between devices, shards(): logits = jnp.sum(lax.all_gather(partial_logits, 'ch'), axis=0)  9.9 us
    convert_element_type x12, other arithmetic, tile_logit(): near_left.astype(jnp.float32)[:, :, None]  9.25 us
    dynamic_update_slice x12, local copies, waits for them, and re-layouts, shards(): lax.scan(tile_step, jnp.zeros((), jnp.float32), (left_feats, right_feats))  7.53 us
    all_to_all x1, starting transfers between devices, shards(): lax.all_to_all(row_send, 'res', split_axis=0, concat_axis=0, tiled=True)  6.45 us
  transfers between devices with their start and end apart: 4, of which 3 were waited for; matrix products, arithmetic and copies ran while one was open for 48% of the time, Pallas kernels for 0%

profile of v1, /device:TPU:0, one launch (start us, length us, event | category | flops | bytes accessed | tf_op | source)
XLA Modules:
  0.0 215.8 jit_solution(16010191906731456781)
XLA Ops:
  7.2 0.7 constant_dynamic-slice_fusion.1
  8.5 2.3 %gather_fusion = bf16[16,128,384]{2,1,0:T(8,128)(2,1)S(1)} fusion(bf16[16,128,384]{2,1,0:T(8,128)(2,1)} %bitcast.220, s32[1024]{0:T(1024)S(1)} %pad_clamp_fusion.1), kind=kCustom, calls=%fused_computation.4 | custom fusion | bytes 3145792 | tf_op jit(solution)/shard_map/jit(_take)/gather | solution.py:116
  10.8 1.4 broadcast_select_fusion
  12.2 6.4 %all-to-all-start = ((bf16[4,4,128,384]{3,2,1,0:T(8,128)(2,1)}), bf16[4,4,128,384]{3,2,1,0:T(8,128)(2,1)S(1)}, u32[]{:S(2)}, u32[]{:S(2)}) async-start(bf16[4,4,128,384]{3,2,1,0:T(8,128)(2,1)} %broadcast_select_fusion), calls=%async_computation | async-start | bytes 3145728 | tf_op jit(solution)/shard_map/all_to_all | solution.py:119
  18.6 0.7 dynamic-slice_bitcast_fusion
  19.9 1.8 gather_fusion.2
  22.0 1.2 gather_fusion.1
  23.2 1.2 gather_fusion.4
  24.5 0.8 convert_reduce_fusion
  25.8 1.7 fusion.42
  27.5 2.5 %convolution_convert_fusion.4 = bf16[12,128,128]{2,1,0:T(8,128)(2,1)} fusion(bf16[12,128,384]{2,1,0:T(8,128)(2,1)} %gather_fusion.2, pred[12]{0:T(512)(128)(4,1)S(1)} %get-tuple-element.81, bf16[384,128]{1,0:T(8,128)(2,1)} %param.25), kind=kOutput, calls=%fused_computation.52 | convolution fusion | flops 151781376 | bytes 1671180 | tf_op jit(solution)/shard_map/pad,dc->pac/dot_general | solution.py:122
  30.0 25.5 %all-to-all-done = bf16[4,4,128,384]{3,2,1,0:T(8,128)(2,1)S(1)} async-done(((bf16[4,4,128,384]{3,2,1,0:T(8,128)(2,1)}), bf16[4,4,128,384]{3,2,1,0:T(8,128)(2,1)S(1)}, u32[]{:S(2)}, u32[]{:S(2)}) %all-to-all-start) | async-done | bytes 1572896 | tf_op jit(solution)/shard_map/all_to_all | solution.py:119
  55.6 3.3 %all-to-all-start.1 = ((bf16[4,4,26,128]{3,1,2,0:T(4,128)(2,1)}), bf16[4,4,26,128]{3,1,2,0:T(4,128)(2,1)S(1)}, u32[]{:S(2)}, u32[]{:S(2)}) async-start(bf16[4,4,26,128]{3,1,2,0:T(4,128)(2,1)} %fusion.42), calls=%async_computation.1 | async-start | bytes 212992 | tf_op jit(solution)/shard_map/all_to_all | solution.py:134
  58.9 1.8 gather_fusion.3
  60.7 1.8 convolution_convert_fusion.3
  62.6 79.4 %while.11 = (s32[]{:T(128)}, f32[12,128,128]{2,1,0:T(8,128)}, bf16[12,128,128]{2,1,0:T(8,128)(2,1)}, bf16[12,128,128]{2,1,0:T(8,128)(2,1)S(1)}, bf16[128,64]{0,1...) while((s32[]{:T(128)}, f32[12,128,128]{2,1,0:T(8,128)}, bf16[12,128,128]{2,1,0:T(8,128)(2,1)}, ...), condition=%wide.region_5.7_spmd.clone, body=%wide.region_4.6_spmd.sunk.clone | while | flops 287342592 | bytes 9061461 | solution.py:143
  62.8 0.8 bitcast_convert_fusion.3
  63.5 2.5 %fusion.98 = f32[128,128,64]{1,2,0:T(8,128)S(1)} fusion(f32[128,128]{1,0:T(8,128)S(1)} %convert_bitcast_fusion.3, f32[128,128]{1,0:T(8,128)S(1)} %bitcast_convert_fusion.3, bf16[128,64]{0,1:T(8,128)(2,1)S(1)} %get-tuple-element.198), kind=kOutput, calls=%fused_computation.7.clone.1.clone | convolution fusion | flops 272629760 | bytes 4341760 | tf_op jit(solution)/shard_map/while/body/eval_jaxpr/kc,akb->acb/dot_general | solution.py:13
  66.1 2.5 %fusion.99 = f32[1,128,128]{2,0,1:T(1,128)S(1)} fusion(f32[128,128,64]{1,2,0:T(8,128)S(1)} %fusion.98, f32[64]{0:T(128)S(1)} %get-tuple-element.199, f32[64]{0:T(128)S(1)} %get-tuple-element.200), kind=kOutput, calls=%fused_computation.8.clone.1.clone | convolution fusion | flops 14680064 | bytes 4260352 | tf_op jit(solution)/shard_map/while/body/eval_jaxpr/c,acb->ab/dot_general | solution.py:15
  69.4 0.8 bitcast_convert_fusion.3
  70.1 2.5 %fusion.98 = f32[128,128,64]{1,2,0:T(8,128)S(1)} fusion(f32[128,128]{1,0:T(8,128)S(1)} %convert_bitcast_fusion.3, f32[128,128]{1,0:T(8,128)S(1)} %bitcast_convert_fusion.3, bf16[128,64]{0,1:T(8,128)(2,1)S(1)} %get-tuple-element.198), kind=kOutput, calls=%fused_computation.7.clone.1.clone | convolution fusion | flops 272629760 | bytes 4341760 | tf_op jit(solution)/shard_map/while/body/eval_jaxpr/kc,akb->acb/dot_general | solution.py:13
  72.7 2.5 %fusion.99 = f32[1,128,128]{2,0,1:T(1,128)S(1)} fusion(f32[128,128,64]{1,2,0:T(8,128)S(1)} %fusion.98, f32[64]{0:T(128)S(1)} %get-tuple-element.199, f32[64]{0:T(128)S(1)} %get-tuple-element.200), kind=kOutput, calls=%fused_computation.8.clone.1.clone | convolution fusion | flops 14680064 | bytes 4260352 | tf_op jit(solution)/shard_map/while/body/eval_jaxpr/c,acb->ab/dot_general | solution.py:15
  76.0 0.8 bitcast_convert_fusion.3
  76.8 2.5 %fusion.98 = f32[128,128,64]{1,2,0:T(8,128)S(1)} fusion(f32[128,128]{1,0:T(8,128)S(1)} %convert_bitcast_fusion.3, f32[128,128]{1,0:T(8,128)S(1)} %bitcast_convert_fusion.3, bf16[128,64]{0,1:T(8,128)(2,1)S(1)} %get-tuple-element.198), kind=kOutput, calls=%fused_computation.7.clone.1.clone | convolution fusion | flops 272629760 | bytes 4341760 | tf_op jit(solution)/shard_map/while/body/eval_jaxpr/kc,akb->acb/dot_general | solution.py:13
  79.3 2.5 %fusion.99 = f32[1,128,128]{2,0,1:T(1,128)S(1)} fusion(f32[128,128,64]{1,2,0:T(8,128)S(1)} %fusion.98, f32[64]{0:T(128)S(1)} %get-tuple-element.199, f32[64]{0:T(128)S(1)} %get-tuple-element.200), kind=kOutput, calls=%fused_computation.8.clone.1.clone | convolution fusion | flops 14680064 | bytes 4260352 | tf_op jit(solution)/shard_map/while/body/eval_jaxpr/c,acb->ab/dot_general | solution.py:15
  82.6 0.8 bitcast_convert_fusion.3
  83.4 2.5 %fusion.98 = f32[128,128,64]{1,2,0:T(8,128)S(1)} fusion(f32[128,128]{1,0:T(8,128)S(1)} %convert_bitcast_fusion.3, f32[128,128]{1,0:T(8,128)S(1)} %bitcast_convert_fusion.3, bf16[128,64]{0,1:T(8,128)(2,1)S(1)} %get-tuple-element.198), kind=kOutput, calls=%fused_computation.7.clone.1.clone | convolution fusion | flops 272629760 | bytes 4341760 | tf_op jit(solution)/shard_map/while/body/eval_jaxpr/kc,akb->acb/dot_general | solution.py:13
  85.9 2.5 %fusion.99 = f32[1,128,128]{2,0,1:T(1,128)S(1)} fusion(f32[128,128,64]{1,2,0:T(8,128)S(1)} %fusion.98, f32[64]{0:T(128)S(1)} %get-tuple-element.199, f32[64]{0:T(128)S(1)} %get-tuple-element.200), kind=kOutput, calls=%fused_computation.8.clone.1.clone | convolution fusion | flops 14680064 | bytes 4260352 | tf_op jit(solution)/shard_map/while/body/eval_jaxpr/c,acb->ab/dot_general | solution.py:15
  89.2 0.8 bitcast_convert_fusion.3
  90.0 2.5 %fusion.98 = f32[128,128,64]{1,2,0:T(8,128)S(1)} fusion(f32[128,128]{1,0:T(8,128)S(1)} %convert_bitcast_fusion.3, f32[128,128]{1,0:T(8,128)S(1)} %bitcast_convert_fusion.3, bf16[128,64]{0,1:T(8,128)(2,1)S(1)} %get-tuple-element.198), kind=kOutput, calls=%fused_computation.7.clone.1.clone | convolution fusion | flops 272629760 | bytes 4341760 | tf_op jit(solution)/shard_map/while/body/eval_jaxpr/kc,akb->acb/dot_general | solution.py:13
  92.5 2.5 %fusion.99 = f32[1,128,128]{2,0,1:T(1,128)S(1)} fusion(f32[128,128,64]{1,2,0:T(8,128)S(1)} %fusion.98, f32[64]{0:T(128)S(1)} %get-tuple-element.199, f32[64]{0:T(128)S(1)} %get-tuple-element.200), kind=kOutput, calls=%fused_computation.8.clone.1.clone | convolution fusion | flops 14680064 | bytes 4260352 | tf_op jit(solution)/shard_map/while/body/eval_jaxpr/c,acb->ab/dot_general | solution.py:15
  95.1 0.6 constant_dynamic-update-slice_fusion.3
  95.8 0.8 bitcast_convert_fusion.3
  96.6 2.5 %fusion.98 = f32[128,128,64]{1,2,0:T(8,128)S(1)} fusion(f32[128,128]{1,0:T(8,128)S(1)} %convert_bitcast_fusion.3, f32[128,128]{1,0:T(8,128)S(1)} %bitcast_convert_fusion.3, bf16[128,64]{0,1:T(8,128)(2,1)S(1)} %get-tuple-element.198), kind=kOutput, calls=%fused_computation.7.clone.1.clone | convolution fusion | flops 272629760 | bytes 4341760 | tf_op jit(solution)/shard_map/while/body/eval_jaxpr/kc,akb->acb/dot_general | solution.py:13
  99.1 2.5 %fusion.99 = f32[1,128,128]{2,0,1:T(1,128)S(1)} fusion(f32[128,128,64]{1,2,0:T(8,128)S(1)} %fusion.98, f32[64]{0:T(128)S(1)} %get-tuple-element.199, f32[64]{0:T(128)S(1)} %get-tuple-element.200), kind=kOutput, calls=%fused_computation.8.clone.1.clone | convolution fusion | flops 14680064 | bytes 4260352 | tf_op jit(solution)/shard_map/while/body/eval_jaxpr/c,acb->ab/dot_general | solution.py:15
  102.5 0.8 bitcast_convert_fusion.3
  103.2 2.5 %fusion.98 = f32[128,128,64]{1,2,0:T(8,128)S(1)} fusion(f32[128,128]{1,0:T(8,128)S(1)} %convert_bitcast_fusion.3, f32[128,128]{1,0:T(8,128)S(1)} %bitcast_convert_fusion.3, bf16[128,64]{0,1:T(8,128)(2,1)S(1)} %get-tuple-element.198), kind=kOutput, calls=%fused_computation.7.clone.1.clone | convolution fusion | flops 272629760 | bytes 4341760 | tf_op jit(solution)/shard_map/while/body/eval_jaxpr/kc,akb->acb/dot_general | solution.py:13
  105.8 2.5 %fusion.99 = f32[1,128,128]{2,0,1:T(1,128)S(1)} fusion(f32[128,128,64]{1,2,0:T(8,128)S(1)} %fusion.98, f32[64]{0:T(128)S(1)} %get-tuple-element.199, f32[64]{0:T(128)S(1)} %get-tuple-element.200), kind=kOutput, calls=%fused_computation.8.clone.1.clone | convolution fusion | flops 14680064 | bytes 4260352 | tf_op jit(solution)/shard_map/while/body/eval_jaxpr/c,acb->ab/dot_general | solution.py:15
  109.1 0.8 bitcast_convert_fusion.3
  109.8 2.5 %fusion.98 = f32[128,128,64]{1,2,0:T(8,128)S(1)} fusion(f32[128,128]{1,0:T(8,128)S(1)} %convert_bitcast_fusion.3, f32[128,128]{1,0:T(8,128)S(1)} %bitcast_convert_fusion.3, bf16[128,64]{0,1:T(8,128)(2,1)S(1)} %get-tuple-element.198), kind=kOutput, calls=%fused_computation.7.clone.1.clone | convolution fusion | flops 272629760 | bytes 4341760 | tf_op jit(solution)/shard_map/while/body/eval_jaxpr/kc,akb->acb/dot_general | solution.py:13
  112.4 2.5 %fusion.99 = f32[1,128,128]{2,0,1:T(1,128)S(1)} fusion(f32[128,128,64]{1,2,0:T(8,128)S(1)} %fusion.98, f32[64]{0:T(128)S(1)} %get-tuple-element.199, f32[64]{0:T(128)S(1)} %get-tuple-element.200), kind=kOutput, calls=%fused_computation.8.clone.1.clone | convolution fusion | flops 14680064 | bytes 4260352 | tf_op jit(solution)/shard_map/while/body/eval_jaxpr/c,acb->ab/dot_general | solution.py:15
  115.7 0.8 bitcast_convert_fusion.3
  116.5 2.5 %fusion.98 = f32[128,128,64]{1,2,0:T(8,128)S(1)} fusion(f32[128,128]{1,0:T(8,128)S(1)} %convert_bitcast_fusion.3, f32[128,128]{1,0:T(8,128)S(1)} %bitcast_convert_fusion.3, bf16[128,64]{0,1:T(8,128)(2,1)S(1)} %get-tuple-element.198), kind=kOutput, calls=%fused_computation.7.clone.1.clone | convolution fusion | flops 272629760 | bytes 4341760 | tf_op jit(solution)/shard_map/while/body/eval_jaxpr/kc,akb->acb/dot_general | solution.py:13
  119.0 2.5 %fusion.99 = f32[1,128,128]{2,0,1:T(1,128)S(1)} fusion(f32[128,128,64]{1,2,0:T(8,128)S(1)} %fusion.98, f32[64]{0:T(128)S(1)} %get-tuple-element.199, f32[64]{0:T(128)S(1)} %get-tuple-element.200), kind=kOutput, calls=%fused_computation.8.clone.1.clone | convolution fusion | flops 14680064 | bytes 4260352 | tf_op jit(solution)/shard_map/while/body/eval_jaxpr/c,acb->ab/dot_general | solution.py:15
  121.5 0.6 constant_dynamic-update-slice_fusion.3
  122.3 0.8 bitcast_convert_fusion.3
  123.1 2.5 %fusion.98 = f32[128,128,64]{1,2,0:T(8,128)S(1)} fusion(f32[128,128]{1,0:T(8,128)S(1)} %convert_bitcast_fusion.3, f32[128,128]{1,0:T(8,128)S(1)} %bitcast_convert_fusion.3, bf16[128,64]{0,1:T(8,128)(2,1)S(1)} %get-tuple-element.198), kind=kOutput, calls=%fused_computation.7.clone.1.clone | convolution fusion | flops 272629760 | bytes 4341760 | tf_op jit(solution)/shard_map/while/body/eval_jaxpr/kc,akb->acb/dot_general | solution.py:13
  125.6 2.5 %fusion.99 = f32[1,128,128]{2,0,1:T(1,128)S(1)} fusion(f32[128,128,64]{1,2,0:T(8,128)S(1)} %fusion.98, f32[64]{0:T(128)S(1)} %get-tuple-element.199, f32[64]{0:T(128)S(1)} %get-tuple-element.200), kind=kOutput, calls=%fused_computation.8.clone.1.clone | convolution fusion | flops 14680064 | bytes 4260352 | tf_op jit(solution)/shard_map/while/body/eval_jaxpr/c,acb->ab/dot_general | solution.py:15
  128.9 0.8 bitcast_convert_fusion.3
  129.7 2.5 %fusion.98 = f32[128,128,64]{1,2,0:T(8,128)S(1)} fusion(f32[128,128]{1,0:T(8,128)S(1)} %convert_bitcast_fusion.3, f32[128,128]{1,0:T(8,128)S(1)} %bitcast_convert_fusion.3, bf16[128,64]{0,1:T(8,128)(2,1)S(1)} %get-tuple-element.198), kind=kOutput, calls=%fused_computation.7.clone.1.clone | convolution fusion | flops 272629760 | bytes 4341760 | tf_op jit(solution)/shard_map/while/body/eval_jaxpr/kc,akb->acb/dot_general | solution.py:13
  132.2 2.6 %fusion.99 = f32[1,128,128]{2,0,1:T(1,128)S(1)} fusion(f32[128,128,64]{1,2,0:T(8,128)S(1)} %fusion.98, f32[64]{0:T(128)S(1)} %get-tuple-element.199, f32[64]{0:T(128)S(1)} %get-tuple-element.200), kind=kOutput, calls=%fused_computation.8.clone.1.clone | convolution fusion | flops 14680064 | bytes 4260352 | tf_op jit(solution)/shard_map/while/body/eval_jaxpr/c,acb->ab/dot_general | solution.py:15
  135.6 0.8 bitcast_convert_fusion.3
  136.3 2.5 %fusion.98 = f32[128,128,64]{1,2,0:T(8,128)S(1)} fusion(f32[128,128]{1,0:T(8,128)S(1)} %convert_bitcast_fusion.3, f32[128,128]{1,0:T(8,128)S(1)} %bitcast_convert_fusion.3, bf16[128,64]{0,1:T(8,128)(2,1)S(1)} %get-tuple-element.198), kind=kOutput, calls=%fused_computation.7.clone.1.clone | convolution fusion | flops 272629760 | bytes 4341760 | tf_op jit(solution)/shard_map/while/body/eval_jaxpr/kc,akb->acb/dot_general | solution.py:13
  138.9 2.5 %fusion.99 = f32[1,128,128]{2,0,1:T(1,128)S(1)} fusion(f32[128,128,64]{1,2,0:T(8,128)S(1)} %fusion.98, f32[64]{0:T(128)S(1)} %get-tuple-element.199, f32[64]{0:T(128)S(1)} %get-tuple-element.200), kind=kOutput, calls=%fused_computation.8.clone.1.clone | convolution fusion | flops 14680064 | bytes 4260352 | tf_op jit(solution)/shard_map/while/body/eval_jaxpr/c,acb->ab/dot_general | solution.py:15
  143.5 9.9 %all-gather.3.cloned.1.call-done = f32[24,128,128]{2,1,0:T(8,128)} async-done(((f32[12,128,128]{2,1,0:T(8,128)}), f32[24,128,128]{2,1,0:T(8,128)}) %all-gather.3.cloned.1.call-update) | async-done | bytes 1572880 | tf_op jit(solution)/shard_map/all_gather | solution.py:146
  153.4 1.6 reduce_sum.51
  155.0 2.2 %fusion.12 = bf16[12,128,128]{2,1,0:T(8,128)(2,1)S(1)} fusion(bf16[12,128,384]{2,1,0:T(8,128)(2,1)} %gather_fusion.2, pred[12]{0:T(512)(128)(4,1)S(1)} %get-tuple-element.81, bf16[384,128]{1,0:T(8,128)(2,1)S(1)} %copy-done.11, f32[12,128,128]{2,1,0:T(8,128)S(1)} %reduce_sum.51, f32[12,128]{1,0:T(8,128)S(1)} %bitcast.265, f32[12,128]{1,0:T(8,128)S(1)} %bitcast.249, ...), kind=kOutput, calls=%fused_computation.47 | convolution fusion | flops 204079104 | bytes 2482188 | tf_op jit(solution)/shard_map/pab,pac->pbc/dot_general | solution.py:42
  157.6 1.0 copy.48
  158.5 4.9 %all-to-all-start.2 = ((bf16[4,4,128,128]{3,1,2,0:T(4,128)(2,1)}), bf16[4,4,128,128]{3,1,2,0:T(4,128)(2,1)S(1)}, u32[]{:S(2)}, u32[]{:S(2)}) async-start(bf16[4,4,128,128]{3,1,2,0:T(4,128)(2,1)} %copy.48), calls=%async_computation.2 | async-start | bytes 1048576 | tf_op jit(solution)/shard_map/all_to_all | solution.py:155
  163.4 6.3 %fusion.38 = f32[12]{0:T(128)S(1)} fusion(f32[12,128]{1,0:T(8,128)S(1)} %bitcast.235, f32[12,128]{1,0:T(8,128)S(1)} %bitcast.236, f32[12,128]{1,0:T(8,128)S(1)} %bitcast.237, f32[12,128]{1,0:T(8,128)S(1)} %bitcast.238, f32[12,128]{1,0:T(8,128)S(1)} %bitcast.239, f32[12,128]{1,0:T(8,128)S(1)} %bitcast.240, f32[12,128]{1,0:T(8,128)S(1)} %bitcast.241, ...), kind=kLoop, calls=%fused_computation.80 | loop fusion | flops 10813428 | bytes 995376 | tf_op jit(solution)/shard_map/reduce_sum | solution.py:54
  170.2 2.1 fusion.13
  172.3 6.1 %all-to-all-done.2 = bf16[4,4,128,128]{3,1,2,0:T(4,128)(2,1)S(1)} async-done(((bf16[4,4,128,128]{3,1,2,0:T(4,128)(2,1)}), bf16[4,4,128,128]{3,1,2,0:T(4,128)(2,1)S(1)}, u32[]{:S(2)}, u32[]{:S(2)}) %all-to-all-start.2) | async-done | bytes 524320 | tf_op jit(solution)/shard_map/all_to_all | solution.py:155
  179.5 27.7 %all-reduce.1 = bf16[2048,128]{1,0:T(8,128)(2,1)S(1)} all-reduce(f32[2048,128]{1,0:T(8,128)S(1)} %bitcast.225), channel_id=1, replica_groups=mesh['groups'=2,'res'=4,'blk'=2,'ch'=2] {'blk'}, use_global_device_ids=true, to_apply=%region_7.10 | all-reduce | flops 262144 | bytes 1572864 | tf_op jit(solution)/shard_map/psum | solution.py:171
  207.2 1.7 add_convert_fusion
  (149 shorter events, 12.9 us)
Async XLA Ops:
  7.2 200.1 %copy-start = (bf16[128,384]{1,0:T(8,128)(2,1)S(1)}, bf16[128,384]{1,0:T(8,128)(2,1)}, u32[]{:S(2)}) copy-start(bf16[128,384]{1,0:T(8,128)(2,1)} %param.31) | copy-start | bytes 294916
  12.2 7.7 %copy-start.1 = (bf16[2048,384]{1,0:T(8,128)(2,1)S(1)}, bf16[2048,384]{1,0:T(8,128)(2,1)}, u32[]{:S(2)}) copy-start(bf16[2048,384]{1,0:T(8,128)(2,1)} %param.19) | copy-start | bytes 4718596
  12.2 43.4 %all-to-all-start = ((bf16[4,4,128,384]{3,2,1,0:T(8,128)(2,1)}), bf16[4,4,128,384]{3,2,1,0:T(8,128)(2,1)S(1)}, u32[]{:S(2)}, u32[]{:S(2)}) async-start(bf16[4,4,128,384]{3,2,1,0:T(8,128)(2,1)} %broadcast_select_fusion), calls=%async_computation | async-start | bytes 3145728 | tf_op jit(solution)/shard_map/all_to_all | solution.py:119
  18.6 3.1 %copy-start.4 = (f32[12,2048]{1,0:T(8,128)S(1)}, f32[12,2048]{1,0:T(8,128)}, u32[]{:S(2)}) copy-start(f32[12,2048]{1,0:T(8,128)} %param.20) | copy-start | bytes 294916
  18.6 3.1 %copy-start.5 = (f32[12,2048]{1,0:T(8,128)S(1)}, f32[12,2048]{1,0:T(8,128)}, u32[]{:S(2)}) copy-start(f32[12,2048]{1,0:T(8,128)} %param.21) | copy-start | bytes 294916
  19.9 2.0 copy-start.8
  19.9 2.0 copy-start.9
  30.0 30.7 %copy-start.10 = (bf16[384,128]{1,0:T(8,128)(2,1)S(1)}, bf16[384,128]{1,0:T(8,128)(2,1)}, u32[]{:S(2)}) copy-start(bf16[384,128]{1,0:T(8,128)(2,1)} %param.26) | copy-start | bytes 294916
  55.6 87.1 %all-to-all-start.1 = ((bf16[4,4,26,128]{3,1,2,0:T(4,128)(2,1)}), bf16[4,4,26,128]{3,1,2,0:T(4,128)(2,1)S(1)}, u32[]{:S(2)}, u32[]{:S(2)}) async-start(bf16[4,4,26,128]{3,1,2,0:T(4,128)(2,1)} %fusion.42), calls=%async_computation.1 | async-start | bytes 212992 | tf_op jit(solution)/shard_map/all_to_all | solution.py:134
  58.9 94.5 %all-gather.3.cloned.1.call-start = ((), (), s32[]{:S(2)}) async-start(), calls=%async_computation.3 | async-start | bytes 2359296 | tf_op jit(solution)/shard_map/all_gather | solution.py:146
  60.7 1.9 copy-start.3
  60.7 1.9 copy-start.6
  60.7 1.9 copy-start.7
  62.6 79.5 %copy-start.2 = (f32[12,26,128]{2,1,0:T(8,128)S(1)}, f32[12,26,128]{2,1,0:T(8,128)}, u32[]{:S(2)}) copy-start(f32[12,26,128]{2,1,0:T(8,128)} %gather_fusion.4) | copy-start | bytes 479236
  143.3 11.7 %copy-start.11 = (bf16[384,128]{1,0:T(8,128)(2,1)S(1)}, bf16[384,128]{1,0:T(8,128)(2,1)}, u32[]{:S(2)}) copy-start(bf16[384,128]{1,0:T(8,128)(2,1)} %param.27) | copy-start | bytes 294916
  158.5 19.8 %all-to-all-start.2 = ((bf16[4,4,128,128]{3,1,2,0:T(4,128)(2,1)}), bf16[4,4,128,128]{3,1,2,0:T(4,128)(2,1)S(1)}, u32[]{:S(2)}, u32[]{:S(2)}) async-start(bf16[4,4,128,128]{3,1,2,0:T(4,128)(2,1)} %copy.48), calls=%async_computation.2 | async-start | bytes 1048576 | tf_op jit(solution)/shard_map/all_to_all | solution.py:155
Sparse Core Ops, SparseCore 0:
  142.2 11.1 all-gather.2
